TPU v7x, 256 devices: a whole 4x4x8 slice. The times are simulated.
256 devices in a mesh: dp: 32 (over x, z), mp: 8 (over y, core).
Axes of the slice: x: 4, y: 4, z: 8, core: 2. Of those that a mesh axis runs over, the one named last changes fastest.
Arguments:
- teacher_feat: bfloat16 [3072, 256], P('dp'), may hold values from -6 to 6
- student_feat: bfloat16 [15360, 256], P('dp'), may hold values from -6 to 6
- teacher_weight: bfloat16 [256, 65536], P(None, 'mp'), may hold values from -1.5 to 1.5
- student_weight: bfloat16 [256, 65536], P(None, 'mp'), may hold values from -0.375 to 0.375
- crop_to_image: int32 [15360], P('dp'), may hold values from 0 to 95
Outputs:
- feat_grad: float32 [15360, 256], P('dp', 'mp')
- proto_grad: float32 [256, 65536], P('dp', 'mp')
Inputs may be any that keep to these rules, and one draw needn't show every extreme that they name: `crop_to_image`: crop c of the data block d names teacher row d * 96 + crop_to_image_c.
All inputs are finite; a program needn't handle non-finite values.
Results may differ from a plain program's by a relative error of at most 0.0015.
The roundings to bfloat16 on the way count: a program that leaves them out, or rounds other values in their place, can miss the bound.
Values sent between devices are 32-bit elements; how exact they have to be, the bound alone decides.
No kernel may reach another device: no remote copies, remote signals or barrier semaphores. Data moves between devices by JAX's collectives and lax.ppermute only.
A program may use at most 128 MiB of HBM per device.

v0:
```python
import jax
import jax.numpy as jnp
from jax import lax
from jax.sharding import PartitionSpec as P

P_SIZE = 65536
ITERS = 3


eps = 1e-06
t_temp = 0.07
s_temp = 0.1
loss_scale = 1024.0


def row_unit(x):
    values = x.astype(jnp.float32)
    inverse = lax.rsqrt(jnp.sum(values * values, axis=1, keepdims=True) + eps)
    return (values * inverse, inverse)


def col_unit(w):
    values = w.astype(jnp.float32)
    return (values * lax.rsqrt(jnp.sum(values * values, axis=0, keepdims=True) + eps)).astype(
        jnp.bfloat16
    )


def column_pass(q):
    column = lax.psum(jnp.sum(q, axis=0), "dp")
    return q / (column[None, :] * P_SIZE)


def crop_totals(q):
    return lax.psum(jnp.sum(q, axis=1), "mp")


def shards(teacher_feat, student_feat, teacher_weight, student_weight, crop_to_image):
    teacher_total = teacher_feat.shape[0] * lax.axis_size("dp")
    teacher_unit, _ = row_unit(teacher_feat)
    teacher_norm = col_unit(teacher_weight)
    scores = jnp.dot(
        teacher_unit.astype(jnp.bfloat16), teacher_norm, preferred_element_type=jnp.float32
    )
    q = jnp.exp(scores / t_temp)
    student_norm = col_unit(student_weight)
    unit_rows, inverse = row_unit(student_feat)
    unit_bf = unit_rows.astype(jnp.bfloat16)
    logits = jnp.dot(unit_bf, student_norm, preferred_element_type=jnp.float32) / s_temp
    expo = jnp.exp(logits)
    partial_exp = jnp.sum(expo, axis=1)
    for step in range(ITERS):
        q = column_pass(q)
        row_total = crop_totals(q)
        q = q / (row_total[:, None] * teacher_total)
    exp_total = lax.psum(partial_exp, "mp")
    targets = q * teacher_total
    probs = expo / exp_total[:, None]
    picked = jnp.take(targets, crop_to_image, axis=0)
    dlog = (loss_scale * (probs - picked) / s_temp).astype(jnp.bfloat16)
    grad_part = lax.dot_general(
        dlog, student_norm, (((1,), (1,)), ((), ())), preferred_element_type=jnp.float32
    )
    width_share = unit_rows.shape[1] // lax.axis_size("mp")
    grad_rows = lax.psum(grad_part, "mp")
    feat_full = (
        grad_rows - unit_rows * jnp.sum(unit_rows * grad_rows, axis=1, keepdims=True)
    ) * inverse
    feat_grad = lax.dynamic_slice_in_dim(
        feat_full, lax.axis_index("mp") * width_share, width_share, 1
    )
    proto_grad = lax.psum_scatter(
        lax.dot_general(
            unit_bf, dlog, (((0,), (0,)), ((), ())), preferred_element_type=jnp.float32
        ),
        "dp",
        scatter_dimension=0,
        tiled=True,
    )
    return (feat_grad, proto_grad)


def solution(mesh):
    placed = (P("dp", None), P("dp", None), P(None, "mp"), P(None, "mp"), P("dp"))
    return jax.shard_map(
        shards,
        mesh=mesh,
        in_specs=placed,
        out_specs=(P("dp", "mp"), P("dp", "mp")),
        check_vma=False,
    )
```

profile of v0, /device:TPU:8, one launch (start us, length us, event | category | flops | bytes accessed | tf_op | source)
XLA Modules:
  0.0 752.0 jit_solution(6636379560022398261)
XLA Ops:
  8.0 0.0 copy-start.6
  8.0 0.0 all-reduce.3.cloned.1.call-start
  8.1 0.0 copy-start.4
  8.1 0.8 compare_select_fusion
  8.9 0.9 compare_and_fusion
  9.8 3.1 fusion.4
  12.9 0.0 copy-done.6
  12.9 0.1 fusion.29
  13.0 0.0 copy-done.4
  13.0 1.4 fusion.33
  14.4 0.0 copy-start
  14.4 145.7 %psum.57 = f32[8192]{0:T(1024)S(1)} all-reduce(f32[8192]{0:T(1024)S(1)} %get-tuple-element.8), channel_id=1, replica_groups=mesh['dp'=32,'mp'=8] {'dp'}, use_global_device_ids=true, to_apply=%region_7.0 | all-reduce | flops 8192 | bytes 65536 | tf_op jit(solution)/shard_map/psum | solution.py:30
  160.1 0.3 divide_reduce_fusion
  160.5 10.0 %psum.58 = f32[96]{0:T(128)S(1)} all-reduce(f32[96]{0:T(128)S(1)} %divide_reduce_fusion), channel_id=1, replica_groups=mesh['dp'=32,'mp'=8] {'mp'}, use_global_device_ids=true, to_apply=%region_9.0 | all-reduce | flops 96 | bytes 768 | tf_op jit(solution)/shard_map/psum | solution.py:35
  170.5 0.7 fusion.20
  171.1 137.7 %psum.59 = f32[8192]{0:T(1024)S(1)} all-reduce(f32[8192]{0:T(1024)S(1)} %fusion.20), channel_id=1, replica_groups=mesh['dp'=32,'mp'=8] {'dp'}, use_global_device_ids=true, to_apply=%region_11.0 | all-reduce | flops 8192 | bytes 65536 | tf_op jit(solution)/shard_map/psum | solution.py:30
  308.8 0.0 copy-start.5
  308.8 0.7 fusion.21
  309.6 11.8 %psum.60 = f32[96]{0:T(128)S(1)} all-reduce(f32[96]{0:T(128)S(1)} %fusion.21), channel_id=1, replica_groups=mesh['dp'=32,'mp'=8] {'mp'}, use_global_device_ids=true, to_apply=%region_13.0 | all-reduce | flops 96 | bytes 768 | tf_op jit(solution)/shard_map/psum | solution.py:35
  321.4 0.7 fusion.22
  322.1 137.7 %psum.61 = f32[8192]{0:T(1024)S(1)} all-reduce(f32[8192]{0:T(1024)S(1)} %fusion.22), channel_id=1, replica_groups=mesh['dp'=32,'mp'=8] {'dp'}, use_global_device_ids=true, to_apply=%region_15.0 | all-reduce | flops 8192 | bytes 65536 | tf_op jit(solution)/shard_map/psum | solution.py:30
  459.8 0.0 copy-start.2
  459.8 0.0 copy-done
  459.8 0.9 fusion.23
  460.7 0.0 copy-done.5
  460.7 0.1 fusion.24
  460.9 3.2 fusion.2
  464.1 0.0 copy-done.2
  464.1 7.1 fusion
  471.2 12.6 %all-reduce = (f32[96]{0:T(128)S(1)}, f32[480]{0:T(512)S(1)}) all-reduce(f32[96]{0:T(128)S(1)} %fusion.23, f32[480]{0:T(512)S(1)} %get-tuple-element.10), channel_id=1, replica_groups=mesh['dp'=32,'mp'=8] {'mp'}, use_global_device_ids=true, to_apply=%region_17.0 | all-reduce | flops 576 | bytes 4608 | tf_op jit(solution)/shard_map/psum | solution.py:35
  483.8 2.8 fusion.19
  486.6 8.5 %gather_fusion = f32[480,8192]{1,0:T(8,128)} fusion(f32[96,8192]{1,0:T(8,128)S(1)} %fusion.19, s32[1024]{0:T(1024)S(1)} %pad_clamp_fusion), kind=kCustom, calls=%fused_computation | custom fusion | bytes 31459200 | tf_op jit(solution)/shard_map/jit(_take)/gather | solution.py:59
  495.1 0.0 copy-start.3
  495.1 11.5 %multiply_convert_fusion = bf16[480,8192]{1,0:T(8,128)(2,1)S(1)} fusion(f32[480,8192]{1,0:T(8,128)} %gather_fusion, f32[480,8192]{1,0:T(8,128)} %get-tuple-element.11, f32[480]{0:T(512)S(1)} %get-tuple-element.5, pred[480]{0:T(512)(128)(4,1)S(1)} %compare_and_fusion), kind=kLoop, calls=%fused_computation.1 | loop fusion | flops 23592960 | bytes 39324000 | tf_op jit(solution)/shard_map/convert_element_type | solution.py:60
  506.6 0.0 copy-start.1
  506.6 3.1 copy-done.1
  509.7 0.0 copy-done.3
  509.7 3.0 fusion.14
  512.8 0.0 all-reduce.3.cloned.1.call-update
  512.8 0.0 reduce-scatter.2.cloned.1.call-start
  512.8 8.9 %fusion.26 = f32[256,8192]{1,0:T(8,128)} fusion(bf16[480,8192]{1,0:T(8,128)(2,1)} %copy-done.1, bf16[480,256]{1,0:T(8,128)(2,1)S(1)} %copy-done.5, f32[480]{0:T(512)S(1)} %add_rsqrt_fusion.2), kind=kOutput, calls=%fused_computation.41 | convolution fusion | flops 2013634560 | bytes 16500608 | tf_op jit(solution)/shard_map/dot_general | solution.py:73
  521.8 0.0 reduce-scatter.2.cloned.1.call-update
  521.8 49.7 %all-reduce.3.cloned.1.call-done = f32[480,256]{1,0:T(8,128)} async-done(((f32[480,256]{1,0:T(8,128)}), f32[480,256]{1,0:T(8,128)}) %all-reduce.3.cloned.1.call-update) | async-done | bytes 491536 | tf_op jit(solution)/shard_map/psum | solution.py:65
  571.5 1.3 multiply_reduce_fusion
  572.8 1.3 fusion.25
  574.0 0.7 copy.7
  574.8 169.8 %reduce-scatter.2.cloned.1.call-done = f32[8,8192]{1,0:T(8,128)} async-done(((f32[256,8192]{1,0:T(8,128)}), f32[8,8192]{1,0:T(8,128)}) %reduce-scatter.2.cloned.1.call-update) | async-done | bytes 262160 | tf_op jit(solution)/shard_map/reduce_scatter | solution.py:72
  (11 shorter events, 0.1 us)
Async XLA Ops:
  8.0 4.9 copy-start.6
  8.0 563.5 %all-reduce.3.cloned.1.call-start = ((), (), s32[]{:S(2)}) async-start(), calls=%async_computation.1 | async-start | bytes 983040 | tf_op jit(solution)/shard_map/psum | solution.py:65
  8.1 4.9 copy-start.4
  14.4 445.4 %copy-start = (f32[96,8192]{1,0:T(8,128)}, f32[96,8192]{1,0:T(8,128)S(1)}, u32[]{:S(2)}) copy-start(f32[96,8192]{1,0:T(8,128)S(1)} %get-tuple-element.9) | copy-start | bytes 9437188
  308.8 151.9 %copy-start.5 = (bf16[480,256]{1,0:T(8,128)(2,1)S(1)}, bf16[480,256]{1,0:T(8,128)(2,1)}, u32[]{:S(2)}) copy-start(bf16[480,256]{1,0:T(8,128)(2,1)} %param.6) | copy-start | bytes 737284
  459.8 4.3 copy-start.2
  495.1 14.6 %copy-start.3 = (bf16[256,8192]{1,0:T(8,128)(2,1)S(1)}, bf16[256,8192]{1,0:T(8,128)(2,1)}, u32[]{:S(2)}) copy-start(bf16[256,8192]{1,0:T(8,128)(2,1)} %param.8) | copy-start | bytes 12582916
  506.6 3.1 copy-start.1
  512.8 231.8 %reduce-scatter.2.cloned.1.call-start = ((), (), s32[]{:S(2)}) async-start(), calls=%async_computation.2 | async-start | bytes 8650752 | tf_op jit(solution)/shard_map/reduce_scatter | solution.py:72
Sparse Core Ops, SparseCore 0:
  512.9 58.5 all-reduce.2
Sparse Core Ops, SparseCore 1:
  521.9 222.6 reduce-scatter.1
where the time goes:
time: 752 us
  blocking collectives  455 us (61%)
  waiting for transfers between devices  220 us (29%)
  other arithmetic  28.5 us (4%)
  matrix products  20.5 us (3%)
  between operations  15.7 us (2%)
  local copies, waits for them, and re-layouts  12.4 us (2%)
    psum x3, blocking collectives, column_pass(): column = lax.psum(jnp.sum(q, axis=0), 'dp')  421 us
    reduce_scatter x1, waiting for transfers between devices, shards(): lax.psum_scatter(lax.dot_general(unit_bf, dlog, (((0,), (0,)), ((), ())),...  170 us
    psum x1, waiting for transfers between devices, shards(): grad_rows = lax.psum(grad_part, 'mp')  49.7 us
    psum x3, blocking collectives, crop_totals(): return lax.psum(jnp.sum(q, axis=1), 'mp')  34.4 us
  transfers between devices with their start and end apart: 2, of which 2 were waited for; matrix products, arithmetic and copies ran while one was open for 2% of the time, Pallas kernels for 0%

commit v1 on v0

v1 whole, which is shorter than its diff:
```python
import functools

import jax
import jax.numpy as jnp
from jax import lax
from jax.experimental import pallas as pl
from jax.experimental.pallas import tpu as pltpu
from jax.sharding import Mesh
from jax.sharding import PartitionSpec as P

K = 256
P_SIZE = 65536
TB_DEV = 96
TB_TOTAL = 3072
ITERS = 3
SB_DEV = 480
NX, NZ, NY, NC = 4, 8, 4, 2
NROW = NX * NY * NC
COLS = P_SIZE // NROW
LG = COLS // 128
TROWS = NX * TB_DEV
SROWS = NX * SB_DEV
BLK = 512
NB = COLS // BLK

eps = 1e-06
t_temp = 0.07
s_temp = 0.1
loss_scale = 1024.0

f32 = jnp.float32
bf16 = jnp.bfloat16
VMEM_LIMIT = 56 * 1024 * 1024


def unit_scale(v):
    return lax.rsqrt(jnp.sum(v * v, axis=1, keepdims=True) + eps)


def norm_columns(w):
    v = w.astype(f32)
    return (v * lax.rsqrt(jnp.sum(v * v, axis=0, keepdims=True) + eps)).astype(bf16)


def dot(a, b, ca, cb):
    return lax.dot_general(a, b, (((ca,), (cb,)), ((), ())), preferred_element_type=f32)


def lane_groups(v):
    return jnp.concatenate([v[:, 128 * k : 128 * (k + 1)] for k in range(v.shape[1] // 128)], 0)


def teacher_kernel(ix, tf, tw, e_out, c_out, tn_out, tu_out):
    j = pl.program_id(0)

    @pl.when(j == 0)
    def _():
        for x in range(NX):
            v = tf[x, :TB_DEV, :]
            tu_out[x * TB_DEV : (x + 1) * TB_DEV, :] = (v * unit_scale(v)).astype(bf16)

    tn = norm_columns(tw[...])
    tn_out[...] = tn
    e = jnp.exp(dot(tu_out[...], tn, 1, 0) * (1.0 / t_temp))
    e_out[...] = e
    col = lane_groups(jnp.sum(e, axis=0, keepdims=True))
    c_out[...] = jnp.broadcast_to(col[None], c_out.shape)


def teacher_pass(ix, tf_all, tw):
    return pl.pallas_call(
        teacher_kernel,
        grid_spec=pltpu.PrefetchScalarGridSpec(
            num_scalar_prefetch=1,
            grid=(2,),
            in_specs=[
                pl.BlockSpec((NX, TB_DEV + 8, K), lambda j, ix: (0, 0, 0)),
                pl.BlockSpec((K, 1024), lambda j, ix: (0, ix[0] * 2 + j)),
            ],
            out_specs=[
                pl.BlockSpec((TROWS, 1024), lambda j, ix: (0, j)),
                pl.BlockSpec((NZ, 8, 128), lambda j, ix: (0, j, 0)),
                pl.BlockSpec((K, 1024), lambda j, ix: (0, j)),
                pl.BlockSpec((TROWS, K), lambda j, ix: (0, 0)),
            ],
        ),
        out_shape=[
            jax.ShapeDtypeStruct((TROWS, COLS), f32),
            jax.ShapeDtypeStruct((NZ, LG, 128), f32),
            jax.ShapeDtypeStruct((K, COLS), bf16),
            jax.ShapeDtypeStruct((TROWS, K), bf16),
        ],
        compiler_params=pltpu.CompilerParams(vmem_limit_bytes=VMEM_LIMIT),
        name="teacher_scores",
    )(ix, tf_all, tw)


def student_kernel(ix, sf, ci, tu, sw, ub_out, tuc_out, sn_out, rs_out, acc):
    j = pl.program_id(0)

    @pl.when(j == 0)
    def _():
        for x in range(NX):
            rows = slice(x * SB_DEV, (x + 1) * SB_DEV)
            v = sf[x]
            ub_out[rows, :] = (v * unit_scale(v)).astype(bf16)
            pick = lax.broadcasted_iota(jnp.int32, (SB_DEV, TB_DEV), 1) == ci[rows, :]
            pick = jnp.where(pick, 1.0, 0.0).astype(bf16)
            tuc_out[rows, :] = dot(
                pick, tu[x * TB_DEV : (x + 1) * TB_DEV, :], 1, 0
            ).astype(bf16)
        acc[...] = jnp.zeros_like(acc)

    sn = norm_columns(sw[...])
    sn_out[...] = sn
    for x in range(NX):
        rows = slice(x * SB_DEV, (x + 1) * SB_DEV)
        e = jnp.exp(dot(ub_out[rows, :], sn, 1, 0) * (1.0 / s_temp))
        total = e[:, :128]
        for k in range(1, BLK // 128):
            total = total + e[:, 128 * k : 128 * (k + 1)]
        acc[rows, :] += total

    @pl.when(j == NB - 1)
    def _():
        for k in range(SROWS // 128):
            rows = slice(128 * k, 128 * (k + 1))
            rs_out[k : k + 1, :] = jnp.sum(acc[rows, :].T, axis=0, keepdims=True)
        rs_out[SROWS // 128 :, :] = jnp.zeros((1, 128), f32)


def student_pass(ix, sf_all, ci, tu, sw):
    whole = lambda shape: pl.BlockSpec(shape, lambda j, ix: (0,) * len(shape))
    return pl.pallas_call(
        student_kernel,
        grid_spec=pltpu.PrefetchScalarGridSpec(
            num_scalar_prefetch=1,
            grid=(NB,),
            in_specs=[
                whole((NX, SB_DEV, K)),
                whole((SROWS, 1)),
                whole((TROWS, K)),
                pl.BlockSpec((K, BLK), lambda j, ix: (0, ix[0] * NB + j)),
            ],
            out_specs=[
                whole((SROWS, K)),
                whole((SROWS, K)),
                pl.BlockSpec((K, BLK), lambda j, ix: (0, j)),
                whole((16, 128)),
            ],
            scratch_shapes=[pltpu.VMEM((SROWS, 128), f32)],
        ),
        out_shape=[
            jax.ShapeDtypeStruct((SROWS, K), bf16),
            jax.ShapeDtypeStruct((SROWS, K), bf16),
            jax.ShapeDtypeStruct((K, COLS), bf16),
            jax.ShapeDtypeStruct((16, 128), f32),
        ],
        compiler_params=pltpu.CompilerParams(vmem_limit_bytes=VMEM_LIMIT),
        name="student_sums",
    )(ix, sf_all, ci, tu, sw)


def row_kernel(c_parts, e, b_out, r_out):
    b = 1.0 / (jnp.sum(c_parts[...], axis=0) * P_SIZE)
    b_out[...] = b
    acc = e[:, :128] * b[0:1, :]
    for k in range(1, LG):
        acc = acc + e[:, 128 * k : 128 * (k + 1)] * b[k : k + 1, :]
    for k in range(TROWS // 128):
        r = jnp.sum(acc[128 * k : 128 * (k + 1), :].T, axis=0, keepdims=True)
        r_out[:, k : k + 1, :] = jnp.broadcast_to(r[None], (NROW, 1, 128))
    r_out[:, TROWS // 128 :, :] = jnp.zeros((NROW, 8 - TROWS // 128, 128), f32)


def row_pass(c_parts, e):
    return pl.pallas_call(
        row_kernel,
        out_shape=[
            jax.ShapeDtypeStruct((LG, 128), f32),
            jax.ShapeDtypeStruct((NROW, 8, 128), f32),
        ],
        compiler_params=pltpu.CompilerParams(vmem_limit_bytes=VMEM_LIMIT),
        name="row_sums",
    )(c_parts, e)


def col_kernel(r_parts, e, c_out):
    a = 1.0 / (jnp.sum(r_parts[...], axis=0)[:3] * TB_TOTAL)
    wide = jnp.concatenate(
        [jnp.broadcast_to(a[k : k + 1, :], (128, 128)).T for k in range(TROWS // 128)], 0
    )
    for k in range(LG):
        c = jnp.sum(e[:, 128 * k : 128 * (k + 1)] * wide, axis=0, keepdims=True)
        c_out[:, k : k + 1, :] = jnp.broadcast_to(c[None], (NZ, 1, 128))


def col_pass(r_parts, e):
    return pl.pallas_call(
        col_kernel,
        out_shape=jax.ShapeDtypeStruct((NZ, LG, 128), f32),
        compiler_params=pltpu.CompilerParams(vmem_limit_bytes=VMEM_LIMIT),
        name="col_sums",
    )(r_parts, e)


def grad_kernel(ub, tuc, ci, rt, st, b, sn, tn, p_out, g0_out, g1_out, g, coef):
    j = pl.program_id(0)

    @pl.when(j == 0)
    def _():
        lane = lax.broadcasted_iota(jnp.int32, (SB_DEV, TB_DEV), 1)
        for x in range(NX):
            rows = slice(x * SB_DEV, (x + 1) * SB_DEV)
            a = (loss_scale / s_temp) / rt[x : x + 1, :]
            pick = jnp.where(lane == ci[rows, :], jnp.broadcast_to(a, (SB_DEV, TB_DEV)), 0.0)
            coef[rows, 0:1] = jnp.sum(pick, axis=1, keepdims=True)
        for k in range(SROWS // 128):
            rows = slice(128 * k, 128 * (k + 1))
            s = (loss_scale / s_temp) / st[k : k + 1, :]
            coef[rows, 1:2] = jnp.broadcast_to(s, (128, 128)).T[:, 0:1]

    for x in range(NX):
        rows = slice(x * SB_DEV, (x + 1) * SB_DEV)
        p = jnp.exp(dot(ub[rows, :], sn[...], 1, 0) * (1.0 / s_temp)) * coef[rows, 1:2]
        t = jnp.exp(dot(tuc[rows, :], tn[...], 1, 0) * (1.0 / t_temp)) * b[...]
        d = (p - t * coef[rows, 0:1]).astype(bf16)
        part = dot(d, sn[...], 1, 1)
        prod = dot(ub[rows, :], d, 0, 0)

        if x == 0:
            p_out[...] = prod
        else:
            p_out[...] += prod

        @pl.when(j == 0)
        def _():
            g[rows, :] = part

        @pl.when(j > 0)
        def _():
            g[rows, :] += part

    @pl.when(j == NB - 1)
    def _():
        v = g[...]
        g0_out[...] = jnp.concatenate([v[:, 64 * y : 64 * y + 32] for y in range(NY)], 1)
        g1_out[...] = jnp.concatenate([v[:, 64 * y + 32 : 64 * y + 64] for y in range(NY)], 1)


def grad_pass(ub, tuc, ci, rt, st, b, sn, tn):
    whole = lambda shape: pl.BlockSpec(shape, lambda j: (0,) * len(shape))
    cols = lambda rows: pl.BlockSpec((rows, BLK), lambda j: (0, j))
    return pl.pallas_call(
        grad_kernel,
        grid=(NB,),
        in_specs=[
            whole((SROWS, K)),
            whole((SROWS, K)),
            whole((SROWS, 1)),
            whole((NX, TB_DEV)),
            whole((16, 128)),
            cols(1),
            cols(K),
            cols(K),
        ],
        out_specs=[cols(K), whole((SROWS, 128)), whole((SROWS, 128))],
        out_shape=[
            jax.ShapeDtypeStruct((K, COLS), f32),
            jax.ShapeDtypeStruct((SROWS, 128), f32),
            jax.ShapeDtypeStruct((SROWS, 128), f32),
        ],
        scratch_shapes=[pltpu.VMEM((SROWS, K), f32), pltpu.VMEM((SROWS, 128), f32)],
        compiler_params=pltpu.CompilerParams(vmem_limit_bytes=VMEM_LIMIT),
        name="dlog_products",
    )(ub, tuc, ci, rt, st, b, sn, tn)


def shift(v, axis, size, d):
    return lax.ppermute(v, axis, [(i, (i + d) % size) for i in range(size)])


def exchange(v, axes):
    return lax.all_to_all(v, axes, 0, 0, tiled=False)


def gather_x(v, ix):
    out = jnp.zeros((NX,) + v.shape, v.dtype)
    out = lax.dynamic_update_slice(out, v[None], (ix,) + (0,) * v.ndim)
    for d in (1, NX - 1, 2):
        got = shift(v, "x", NX, d)
        out = lax.dynamic_update_slice(out, got[None], ((ix - d) % NX,) + (0,) * v.ndim)
    return out


def proto_scatter(p, iz):
    w = p.reshape(NX, NZ, 8, COLS)

    def part(d):
        return lax.dynamic_slice(w, (0, (iz + d) % NZ, 0, 0), (NX, 1, 8, COLS))[:, 0]

    up = part(4)
    for d in (3, 2, 1):
        up = shift(up, "z", NZ, 1) + part(d)
    down = part(-3)
    for d in (2, 1):
        down = shift(down, "z", NZ, -1) + part(-d)
    total = part(0) + shift(up, "z", NZ, 1) + shift(down, "z", NZ, -1)
    got = exchange(total, ("x",))
    return jnp.concatenate([got[x] for x in range(NX)], axis=1)


def feat_sum(g0, g1, ix, iy, ic):
    keep = jnp.where(ic == 0, g0, g1)
    give = jnp.where(ic == 0, g1, g0)
    half = keep + shift(give, "c", NC, 1)
    w = half.reshape(NX, SB_DEV, 128)

    def part(d):
        return lax.dynamic_slice(w, ((ix + d) % NX, 0, 0), (1, SB_DEV, 128))[0]

    far, mid = part(2), SB_DEV // 2
    got_up = shift(far[:mid], "x", NX, 1)
    got_down = shift(far[mid:], "x", NX, -1)
    up = part(1)
    up = jnp.concatenate([up[:mid] + got_up, up[mid:]], 0)
    down = part(-1)
    down = jnp.concatenate([down[:mid], down[mid:] + got_down], 0)
    total = part(0) + shift(up, "x", NX, 1) + shift(down, "x", NX, -1)
    w = total.reshape(SB_DEV, NY, 32).transpose(1, 0, 2)

    def share(d):
        return lax.dynamic_slice(w, ((iy + d) % NY, 0, 0), (1, SB_DEV, 32))[0]

    out = share(0)
    for d in (1, NY - 1, 2):
        out = out + shift(share(d), "y", NY, d)
    return out


def shards(teacher_feat, student_feat, teacher_weight, student_weight, crop_to_image):
    ix, iz = lax.axis_index("x"), lax.axis_index("z")
    iy, ic = lax.axis_index("y"), lax.axis_index("c")
    ixs = jnp.reshape(ix, (1,)).astype(jnp.int32)
    rows = ("x", "y", "c")

    crops = jnp.pad(crop_to_image.astype(f32), (0, 8 * K - SB_DEV)).reshape(8, K)
    packed = jnp.concatenate([teacher_feat.astype(f32), crops], 0)
    tf_all = exchange(jnp.broadcast_to(packed[None], (NX,) + packed.shape), ("x",))
    sf32 = student_feat.astype(f32)
    sf_all = gather_x(sf32, ix)
    ci = tf_all[:, TB_DEV : TB_DEV + 2, :].reshape(NX, 2 * K)[:, :SB_DEV]
    ci = ci.reshape(SROWS, 1).astype(jnp.int32)

    e, c_parts, tn, tu = teacher_pass(ixs, tf_all, teacher_weight)
    ub, tuc, sn, sums = student_pass(ixs, sf_all, ci, tu, student_weight)

    for step in range(ITERS):
        b, r_parts = row_pass(exchange(c_parts, ("z",)), e)
        if step < ITERS - 1:
            r_parts = exchange(r_parts, rows)
            c_parts = col_pass(r_parts, e)
        else:
            wide = jnp.broadcast_to(sums[None], (NROW, 16, 128))
            both = exchange(jnp.concatenate([r_parts, wide], 1), rows).sum(0)
    rt = both[:3].reshape(NX, TB_DEV)
    proto, g0, g1 = grad_pass(ub, tuc, ci, rt, both[8:], b.reshape(1, COLS), sn, tn)

    proto_grad = proto_scatter(proto, iz)
    g = feat_sum(g0, g1, ix, iy, ic)
    inverse = unit_scale(sf32)
    mine = (iy * NC + ic) * 32
    u = lax.dynamic_slice(sf32, (0, mine), (SB_DEV, 32)) * inverse
    along = jnp.pad(jnp.sum(u * g, axis=1), (0, 1024 - SB_DEV)).reshape(8, 128)
    along = exchange(jnp.broadcast_to(along[None], (NY * NC, 8, 128)), ("y", "c")).sum(0)
    along = along.reshape(1024)[:SB_DEV]
    feat_grad = (g - u * along[:, None]) * inverse
    return (feat_grad, proto_grad)


def solution(mesh):
    split = Mesh(mesh.devices.reshape(NX, NZ, NY, NC), ("x", "z", "y", "c"))
    dp, mp = ("x", "z"), ("y", "c")
    return jax.shard_map(
        shards,
        mesh=split,
        in_specs=(P(dp, None), P(dp, None), P(None, mp), P(None, mp), P(dp)),
        out_specs=(P(dp, mp), P(dp, mp)),
        check_vma=False,
    )
```

time: 752 us -> 228 us (0.30)
  blocking collectives: 455 us -> 0 us
  waiting for transfers between devices: 220 us -> 66.5 us
  starting transfers between devices: 0.08 us -> 76.4 us
  Pallas kernels: 0 us -> 45.7 us
  matrix products: 20.5 us -> 0 us
  between operations: 15.7 us -> 1.32 us
  other arithmetic: 28.5 us -> 16.9 us
    psum x6 -> x0, blocking collectives: 455 us -> none  [the longest x3 421 us: column_pass(): column = lax.psum(jnp.sum(q, axis=0), 'dp')]
    reduce_scatter x1 -> x0, waiting for transfers between devices: 170 us -> none  [shards(): lax.psum_scatter(lax.dot_general(unit_bf, dlog, (((0,), (0,)), ((), ())),...]
    all_to_all x0 -> x9, starting transfers between devices: none -> 51.9 us  [exchange(): return lax.all_to_all(v, axes, 0, 0, tiled=False)]
    psum x1 -> x0, waiting for transfers between devices: 49.7 us -> none  [shards(): grad_rows = lax.psum(grad_part, 'mp')]
    pallas_call x0 -> x8, Pallas kernels: none -> 45.7 us  [the longest x1 19.3 us: grad_pass(): pl.pallas_call(grad_kernel, grid=(NB,), in_specs=[whole((SROWS, K)), whol...]
    all_to_all x0 -> x9, waiting for transfers between devices: none -> 43 us  [exchange(): return lax.all_to_all(v, axes, 0, 0, tiled=False)]
    ppermute x0 -> x18, starting transfers between devices: none -> 24.5 us  [shift(): return lax.ppermute(v, axis, [(i, (i + d) % size) for i in range(size)])]
    ppermute x0 -> x18, waiting for transfers between devices: none -> 23.5 us  [shift(): return lax.ppermute(v, axis, [(i, (i + d) % size) for i in range(size)])]
  transfers between devices with their start and end apart: 2 -> 27, of which waited for: 2 -> 16; matrix products, arithmetic and copies ran while one was open for 2% -> 9% of each run, Pallas kernels for 0% -> 10%
where the time goes in v1:
time: 228 us; the launch traced here: 225 us
  starting transfers between devices  76.4 us (34%)
  waiting for transfers between devices  66.5 us (29%)
  Pallas kernels  45.7 us (20%)
  local copies, waits for them, and re-layouts  17.8 us (8%)
  other arithmetic  16.9 us (7%)
    all_to_all x9, starting transfers between devices, exchange(): return lax.all_to_all(v, axes, 0, 0, tiled=False)  51.9 us
    all_to_all x9, waiting for transfers between devices, exchange(): return lax.all_to_all(v, axes, 0, 0, tiled=False)  43 us
    ppermute x18, starting transfers between devices, shift(): return lax.ppermute(v, axis, [(i, (i + d) % size) for i in range(size)])  24.5 us
    ppermute x18, waiting for transfers between devices, shift(): return lax.ppermute(v, axis, [(i, (i + d) % size) for i in range(size)])  23.5 us
    pallas_call x1, Pallas kernels, grad_pass(): pl.pallas_call(grad_kernel, grid=(NB,), in_specs=[whole((SROWS, K)), whol...  19.3 us
    pallas_call x3, Pallas kernels, row_pass(): pl.pallas_call(row_kernel, out_shape=[jax.ShapeDtypeStruct((LG, 128), f32...  8.66 us
    unnamed x31, local copies, waits for them, and re-layouts  7.99 us
    pallas_call x1, Pallas kernels, student_pass(): pl.pallas_call(student_kernel, grid_spec=pltpu.PrefetchScalarGridSpec(num...  7.91 us
  transfers between devices with their start and end apart: 27, of which 16 were waited for; matrix products, arithmetic and copies ran while one was open for 9% of the time, Pallas kernels for 10%

profile of v1, /device:TPU:8, one launch (start us, length us, event | category | flops | bytes accessed | tf_op | source)
XLA Modules:
  0.0 224.6 jit_solution(15046849498715199572)
XLA Ops:
  3.0 4.3 %all-to-all-start = ((f32[4,104,256]{2,1,0:T(8,128)}), f32[4,104,256]{2,1,0:T(8,128)S(1)}, u32[]{:S(2)}, u32[]{:S(2)}) async-start(f32[4,104,256]{2,1,0:T(8,128)} %broadcast_in_dim.41), calls=%async_computation | async-start | bytes 851968 | tf_op jit(solution)/shard_map/all_to_all | solution.py:284
  8.2 3.6 %collective-permute-start.2 = (f32[480,256]{1,0:T(8,128)S(1)}, f32[480,256]{1,0:T(8,128)}, u32[]{:S(2)}, u32[]{:S(2)}) collective-permute-start(f32[480,256]{1,0:T(8,128)S(1)} %convert_element_type.18), channel_id=1, source_target_pairs={{0,128},{64,192},{128,0},{192,64},{1,129},{65,193},{129,1},{193,65... | collective-permute-start | bytes 1474568 | tf_op jit(solution)/shard_map/ppermute | solution.py:280
  11.9 1.2 collective-permute-start.1
  14.2 3.0 %all-to-all-done.tf = f32[4,104,256]{2,1,0:T(8,128)S(1)} async-done(((f32[4,104,256]{2,1,0:T(8,128)}), f32[4,104,256]{2,1,0:T(8,128)S(1)}, u32[]{:S(2)}, u32[]{:S(2)}) %all-to-all-start) | async-done | bytes 426016 | tf_op jit(solution)/shard_map/all_to_all | solution.py:284
  18.0 3.9 %teacher_scores.1 = (f32[384,2048]{1,0:T(8,128)}, f32[8,16,128]{2,1,0:T(8,128)}, bf16[256,2048]{1,0:T(8,128)(2,1)}, bf16[384,256]{1,0:T(8,128)(2,1)}) custom-call(s32[1]{0:T(128)} %bitcast.ix, f32[4,104,256]{2,1,0:T(8,128)} %copy-done.4, bf16[256,8192]{1,0:T(8,128)(2,1)} %tw.1), custom_call_target="tpu_custom_call" | custom-call | tf_op jit(solution)/shard_map/teacher_scores/pallas_call | solution.py:71
  21.9 8.5 %all-to-all-start.1 = ((f32[8,16,128]{2,1,0:T(8,128)}), f32[8,16,128]{2,1,0:T(8,128)S(1)}, u32[]{:S(2)}, u32[]{:S(2)}) async-start(f32[8,16,128]{2,1,0:T(8,128)} %get-tuple-element.20), calls=%async_computation.1 | async-start | bytes 131072 | tf_op jit(solution)/shard_map/all_to_all | solution.py:284
  31.1 7.6 %all-to-all-done.1.c_parts = f32[8,16,128]{2,1,0:T(8,128)S(1)} async-done(((f32[8,16,128]{2,1,0:T(8,128)}), f32[8,16,128]{2,1,0:T(8,128)S(1)}, u32[]{:S(2)}, u32[]{:S(2)}) %all-to-all-start.1) | async-done | bytes 65568 | tf_op jit(solution)/shard_map/all_to_all | solution.py:284
  39.4 2.9 %row_sums.3 = (f32[16,128]{1,0:T(8,128)}, f32[32,8,128]{2,1,0:T(8,128)}) custom-call(f32[8,16,128]{2,1,0:T(8,128)} %copy-done.9, f32[384,2048]{1,0:T(8,128)} %get-tuple-element.21.e), custom_call_target="tpu_custom_call" | custom-call | tf_op jit(solution)/shard_map/row_sums/pallas_call | solution.py:177
  42.3 13.7 %all-to-all-start.2 = ((f32[32,8,128]{2,1,0:T(8,128)}), f32[32,8,128]{2,1,0:T(8,128)S(1)}, u32[]{:S(2)}, u32[]{:S(2)}) async-start(f32[32,8,128]{2,1,0:T(8,128)} %get-tuple-element.22), calls=%async_computation.2 | async-start | bytes 262144 | tf_op jit(solution)/shard_map/all_to_all | solution.py:284
  56.0 1.9 convert_element_type.23.ci
  57.9 4.7 %all-to-all-done.2.r_parts = f32[32,8,128]{2,1,0:T(8,128)S(1)} async-done(((f32[32,8,128]{2,1,0:T(8,128)}), f32[32,8,128]{2,1,0:T(8,128)S(1)}, u32[]{:S(2)}, u32[]{:S(2)}) %all-to-all-start.2) | async-done | bytes 131104 | tf_op jit(solution)/shard_map/all_to_all | solution.py:284
  63.2 3.0 %col_sums.2 = f32[8,16,128]{2,1,0:T(8,128)} custom-call(f32[32,8,128]{2,1,0:T(8,128)} %copy-done.6, f32[384,2048]{1,0:T(8,128)} %get-tuple-element.21.e), custom_call_target="tpu_custom_call" | custom-call | tf_op jit(solution)/shard_map/col_sums/pallas_call | solution.py:199
  66.2 3.4 %all-to-all-start.3 = ((f32[8,16,128]{2,1,0:T(8,128)}), f32[8,16,128]{2,1,0:T(8,128)S(1)}, u32[]{:S(2)}, u32[]{:S(2)}) async-start(f32[8,16,128]{2,1,0:T(8,128)} %col_sums.2), calls=%async_computation.3 | async-start | bytes 131072 | tf_op jit(solution)/shard_map/all_to_all | solution.py:284
  70.6 7.2 %all-to-all-done.3.c_parts = f32[8,16,128]{2,1,0:T(8,128)S(1)} async-done(((f32[8,16,128]{2,1,0:T(8,128)}), f32[8,16,128]{2,1,0:T(8,128)S(1)}, u32[]{:S(2)}, u32[]{:S(2)}) %all-to-all-start.3) | async-done | bytes 65568 | tf_op jit(solution)/shard_map/all_to_all | solution.py:284
  78.5 2.9 %row_sums.4 = (f32[16,128]{1,0:T(8,128)}, f32[32,8,128]{2,1,0:T(8,128)}) custom-call(f32[8,16,128]{2,1,0:T(8,128)} %copy-done.8, f32[384,2048]{1,0:T(8,128)} %get-tuple-element.21.e), custom_call_target="tpu_custom_call" | custom-call | tf_op jit(solution)/shard_map/row_sums/pallas_call | solution.py:177
  81.3 5.0 %all-to-all-start.4 = ((f32[32,8,128]{2,1,0:T(8,128)}), f32[32,8,128]{2,1,0:T(8,128)S(1)}, u32[]{:S(2)}, u32[]{:S(2)}) async-start(f32[32,8,128]{2,1,0:T(8,128)} %get-tuple-element.23), calls=%async_computation.4 | async-start | bytes 262144 | tf_op jit(solution)/shard_map/all_to_all | solution.py:284
  87.4 5.6 %all-to-all-done.4.r_parts = f32[32,8,128]{2,1,0:T(8,128)S(1)} async-done(((f32[32,8,128]{2,1,0:T(8,128)}), f32[32,8,128]{2,1,0:T(8,128)S(1)}, u32[]{:S(2)}, u32[]{:S(2)}) %all-to-all-start.4) | async-done | bytes 131104 | tf_op jit(solution)/shard_map/all_to_all | solution.py:284
  93.7 3.0 %col_sums.3 = f32[8,16,128]{2,1,0:T(8,128)} custom-call(f32[32,8,128]{2,1,0:T(8,128)} %copy-done.5, f32[384,2048]{1,0:T(8,128)} %get-tuple-element.21.e), custom_call_target="tpu_custom_call" | custom-call | tf_op jit(solution)/shard_map/col_sums/pallas_call | solution.py:199
  96.7 3.4 %all-to-all-start.5 = ((f32[8,16,128]{2,1,0:T(8,128)}), f32[8,16,128]{2,1,0:T(8,128)S(1)}, u32[]{:S(2)}, u32[]{:S(2)}) async-start(f32[8,16,128]{2,1,0:T(8,128)} %col_sums.3), calls=%async_computation.5 | async-start | bytes 131072 | tf_op jit(solution)/shard_map/all_to_all | solution.py:284
  101.1 1.3 copy-done
  102.4 7.9 %student_sums.1 = (bf16[1920,256]{1,0:T(8,128)(2,1)}, bf16[1920,256]{1,0:T(8,128)(2,1)}, bf16[256,2048]{1,0:T(8,128)(2,1)}, f32[16,128]{1,0:T(8,128)}) custom-call(s32[1]{0:T(128)} %bitcast.ix, f32[4,480,256]{2,1,0:T(8,128)} %copy-done, s32[1920,1]{1,0:T(8,128)} %convert_element_type.23.ci, bf16[384,256]{1,0:T(8,128)(2,1)} %get-tuple-element.17.tu, ...), custom_call_target="tpu_custom_call" | custom-call | tf_op jit(solution)/shard_map/student_sums/pallas_call | solution.py:134
  110.9 2.9 %row_sums.5 = (f32[16,128]{1,0:T(8,128)}, f32[32,8,128]{2,1,0:T(8,128)}) custom-call(f32[8,16,128]{2,1,0:T(8,128)} %copy-done.7, f32[384,2048]{1,0:T(8,128)} %get-tuple-element.21.e), custom_call_target="tpu_custom_call" | custom-call | tf_op jit(solution)/shard_map/row_sums/pallas_call | solution.py:177
  113.8 1.7 pad_maximum_fusion
  115.5 5.0 %all-to-all-start.6 = ((f32[32,24,128]{2,1,0:T(8,128)}), f32[32,24,128]{2,1,0:T(8,128)S(1)}, u32[]{:S(2)}, u32[]{:S(2)}) async-start(f32[32,24,128]{2,1,0:T(8,128)} %pad_maximum_fusion), calls=%async_computation.6 | async-start | bytes 786432 | tf_op jit(solution)/shard_map/all_to_all | solution.py:284
  120.6 8.7 %all-to-all-done.6 = f32[32,24,128]{2,1,0:T(8,128)S(1)} async-done(((f32[32,24,128]{2,1,0:T(8,128)}), f32[32,24,128]{2,1,0:T(8,128)S(1)}, u32[]{:S(2)}, u32[]{:S(2)}) %all-to-all-start.6) | async-done | bytes 393248 | tf_op jit(solution)/shard_map/all_to_all | solution.py:284
  130.7 19.3 %dlog_products.1 = (f32[256,2048]{1,0:T(8,128)}, f32[1920,128]{1,0:T(8,128)}, f32[1920,128]{1,0:T(8,128)}) custom-call(bf16[1920,256]{1,0:T(8,128)(2,1)} %get-tuple-element.18.ub, bf16[1920,256]{1,0:T(8,128)(2,1)} %get-tuple-element.19.tuc, s32[1920,1]{1,0:T(8,128)} %convert_element_type.23.ci, f32[4,96]{1,0:T(4,128)} %reshape.72.rt, f32[16,128]{1,0:T(8,128)} %slice.87.st, ...), custom_call_target="tpu_custom_call" | custom-call | tf_op jit(solution)/shard_map/dlog_products/pallas_call | solution.py:254
  151.0 2.0 collective-permute-start.11
  153.0 1.3 collective-permute-start.15
  154.4 2.3 %broadcast_select_fusion = f32[1920,128]{1,0:T(8,128)} fusion(f32[1920,128]{1,0:T(8,128)} %get-tuple-element.30, f32[1920,128]{1,0:T(8,128)} %get-tuple-element.29, pred[]{:T(512)S(6)} %eq.24), kind=kLoop, calls=%fused_computation.6 | loop fusion | flops 245760 | bytes 2949121 | tf_op jit(solution)/shard_map/jit(_where)/select_n | solution.py:315
  156.9 4.4 %collective-permute-done.11 = f32[4,8,2048]{2,1,0:T(8,128)S(1)} collective-permute-done((f32[4,8,2048]{2,1,0:T(8,128)S(1)}, f32[4,8,2048]{2,1,0:T(8,128)S(1)}, u32[]{:S(2)}, u32[]{:S(2)}) %collective-permute-start.11) | collective-permute-done | bytes 262176 | tf_op jit(solution)/shard_map/ppermute | solution.py:280
  161.3 1.7 bitcast_add_fusion.4
  163.8 8.7 %collective-permute-done.12 = f32[4,8,2048]{2,1,0:T(8,128)S(1)} collective-permute-done((f32[4,8,2048]{2,1,0:T(8,128)}, f32[4,8,2048]{2,1,0:T(8,128)S(1)}, u32[]{:S(2)}, u32[]{:S(2)}) %collective-permute-start.12) | collective-permute-done | bytes 262176 | tf_op jit(solution)/shard_map/ppermute | solution.py:280
  172.5 1.9 bitcast_add_fusion.3
  174.4 3.2 %collective-permute-start.16 = (f32[4,8,2048]{2,1,0:T(8,128)}, f32[4,8,2048]{2,1,0:T(8,128)}, u32[]{:S(2)}, u32[]{:S(2)}) collective-permute-start(f32[4,8,2048]{2,1,0:T(8,128)} %get-tuple-element.43), channel_id=1, source_target_pairs={{0,56},{8,0},{16,8},{24,16},{32,24},{40,32},{48,40},{56,48},{1,57}... | collective-permute-start | bytes 786440 | tf_op jit(solution)/shard_map/ppermute | solution.py:280
  177.7 1.3 select_add_fusion
  180.2 3.0 %collective-permute-done.13 = f32[4,8,2048]{2,1,0:T(8,128)} collective-permute-done((f32[4,8,2048]{2,1,0:T(8,128)}, f32[4,8,2048]{2,1,0:T(8,128)}, u32[]{:S(2)}, u32[]{:S(2)}) %collective-permute-start.13) | collective-permute-done | bytes 262176 | tf_op jit(solution)/shard_map/ppermute | solution.py:280
  183.2 1.9 bitcast_add_fusion.2
  185.4 3.0 %collective-permute-start.17 = (f32[4,8,2048]{2,1,0:T(8,128)S(1)}, f32[4,8,2048]{2,1,0:T(8,128)}, u32[]{:S(2)}, u32[]{:S(2)}) collective-permute-start(f32[4,8,2048]{2,1,0:T(8,128)S(1)} %get-tuple-element.41), channel_id=1, source_target_pairs={{0,56},{8,0},{16,8},{24,16},{32,24},{40,32},{48,40},{56,48},{1,57}... | collective-permute-start | bytes 786440 | tf_op jit(solution)/shard_map/ppermute | solution.py:280
  189.0 1.8 collective-permute-start.6
  191.4 3.1 %collective-permute-done.6 = f32[240,128]{0,1:T(8,128)S(1)} collective-permute-done((f32[240,128]{0,1:T(8,128)S(1)}, f32[240,128]{0,1:T(8,128)S(1)}, u32[]{:S(2)}, u32[]{:S(2)}) %collective-permute-start.6) | collective-permute-done | bytes 122912 | tf_op jit(solution)/shard_map/ppermute | solution.py:280
  194.6 2.6 %collective-permute-start.7 = (f32[480,128]{0,1:T(8,128)S(1)}, f32[480,128]{0,1:T(8,128)S(1)}, u32[]{:S(2)}, u32[]{:S(2)}) collective-permute-start(f32[480,128]{0,1:T(8,128)S(1)} %pad_maximum_fusion.2), channel_id=1, source_target_pairs={{0,192},{64,0},{128,64},{192,128},{1,193},{65,1},{129,65},{193,129... | collective-permute-start | bytes 737288 | tf_op jit(solution)/shard_map/ppermute | solution.py:280
  197.2 1.8 fusion
  199.0 3.4 %all-to-all-start.8 = ((f32[4,8,2048]{2,1,0:T(8,128)}), f32[4,8,2048]{2,1,0:T(8,128)S(1)}, u32[]{:S(2)}, u32[]{:S(2)}) async-start(f32[4,8,2048]{2,1,0:T(8,128)} %fusion), calls=%async_computation.8 | async-start | bytes 524288 | tf_op jit(solution)/shard_map/all_to_all | solution.py:284
  203.1 2.0 collective-permute-start.9
  206.3 2.8 %all-to-all-done.8 = f32[4,8,2048]{2,1,0:T(8,128)S(1)} async-done(((f32[4,8,2048]{2,1,0:T(8,128)}), f32[4,8,2048]{2,1,0:T(8,128)S(1)}, u32[]{:S(2)}, u32[]{:S(2)}) %all-to-all-start.8) | async-done | bytes 262176 | tf_op jit(solution)/shard_map/all_to_all | solution.py:284
  210.8 2.6 %collective-permute-done.10 = f32[480,32]{1,0:T(8,128)S(1)} collective-permute-done((f32[480,32]{1,0:T(8,128)S(1)}, f32[480,32]{1,0:T(8,128)S(1)}, u32[]{:S(2)}, u32[]{:S(2)}) %collective-permute-start.10) | collective-permute-done | bytes 61472 | tf_op jit(solution)/shard_map/ppermute | solution.py:280
  214.3 5.3 %all-to-all-start.7 = ((f32[8,8,128]{2,1,0:T(8,128)}), f32[8,8,128]{2,1,0:T(8,128)S(1)}, u32[]{:S(2)}, u32[]{:S(2)}) async-start(f32[8,8,128]{2,1,0:T(8,128)} %broadcast_in_dim.44), calls=%async_computation.7 | async-start | bytes 65536 | tf_op jit(solution)/shard_map/all_to_all | solution.py:284
  220.3 3.3 %all-to-all-done.7 = f32[8,8,128]{2,1,0:T(8,128)S(1)} async-done(((f32[8,8,128]{2,1,0:T(8,128)}), f32[8,8,128]{2,1,0:T(8,128)S(1)}, u32[]{:S(2)}, u32[]{:S(2)}) %all-to-all-start.7) | async-done | bytes 32800 | tf_op jit(solution)/shard_map/all_to_all | solution.py:284
  (95 shorter events, 24.4 us)
Async XLA Ops:
  2.1 11.9 %copy-start.3 = (bf16[480,256]{1,0:T(8,128)(2,1)S(1)}, bf16[480,256]{1,0:T(8,128)(2,1)}, u32[]{:S(2)}) copy-start(bf16[480,256]{1,0:T(8,128)(2,1)} %param.6) | copy-start | bytes 737284
  3.0 14.2 %all-to-all-start = ((f32[4,104,256]{2,1,0:T(8,128)}), f32[4,104,256]{2,1,0:T(8,128)S(1)}, u32[]{:S(2)}, u32[]{:S(2)}) async-start(f32[4,104,256]{2,1,0:T(8,128)} %broadcast_in_dim.41), calls=%async_computation | async-start | bytes 851968 | tf_op jit(solution)/shard_map/all_to_all | solution.py:284
  8.2 91.8 %collective-permute-start.2 = (f32[480,256]{1,0:T(8,128)S(1)}, f32[480,256]{1,0:T(8,128)}, u32[]{:S(2)}, u32[]{:S(2)}) collective-permute-start(f32[480,256]{1,0:T(8,128)S(1)} %convert_element_type.18), channel_id=1, source_target_pairs={{0,128},{64,192},{128,0},{192,64},{1,129},{65,193},{129,1},{193,65... | collective-permute-start | bytes 1474568 | tf_op jit(solution)/shard_map/ppermute | solution.py:280
  11.9 74.5 %collective-permute-start.1 = (f32[480,256]{1,0:T(8,128)S(1)}, f32[480,256]{1,0:T(8,128)}, u32[]{:S(2)}, u32[]{:S(2)}) collective-permute-start(f32[480,256]{1,0:T(8,128)S(1)} %convert_element_type.18), channel_id=1, source_target_pairs={{0,192},{64,0},{128,64},{192,128},{1,193},{65,1},{129,65},{193,129... | collective-permute-start | bytes 1474568 | tf_op jit(solution)/shard_map/ppermute | solution.py:280
  13.0 56.5 %collective-permute-start = (f32[480,256]{1,0:T(8,128)S(1)}, f32[480,256]{1,0:T(8,128)}, u32[]{:S(2)}, u32[]{:S(2)}) collective-permute-start(f32[480,256]{1,0:T(8,128)S(1)} %convert_element_type.18), channel_id=1, source_target_pairs={{0,64},{64,128},{128,192},{192,0},{1,65},{65,129},{129,193},{193,1... | collective-permute-start | bytes 1474568 | tf_op jit(solution)/shard_map/ppermute | solution.py:280
  17.2 0.8 copy-start.4
  21.9 16.8 %all-to-all-start.1 = ((f32[8,16,128]{2,1,0:T(8,128)}), f32[8,16,128]{2,1,0:T(8,128)S(1)}, u32[]{:S(2)}, u32[]{:S(2)}) async-start(f32[8,16,128]{2,1,0:T(8,128)} %get-tuple-element.20), calls=%async_computation.1 | async-start | bytes 131072 | tf_op jit(solution)/shard_map/all_to_all | solution.py:284
  38.7 0.6 copy-start.9
  42.3 20.3 %all-to-all-start.2 = ((f32[32,8,128]{2,1,0:T(8,128)}), f32[32,8,128]{2,1,0:T(8,128)S(1)}, u32[]{:S(2)}, u32[]{:S(2)}) async-start(f32[32,8,128]{2,1,0:T(8,128)} %get-tuple-element.22), calls=%async_computation.2 | async-start | bytes 262144 | tf_op jit(solution)/shard_map/all_to_all | solution.py:284
  62.5 0.7 copy-start.6
  66.2 11.7 %all-to-all-start.3 = ((f32[8,16,128]{2,1,0:T(8,128)}), f32[8,16,128]{2,1,0:T(8,128)S(1)}, u32[]{:S(2)}, u32[]{:S(2)}) async-start(f32[8,16,128]{2,1,0:T(8,128)} %col_sums.2), calls=%async_computation.3 | async-start | bytes 131072 | tf_op jit(solution)/shard_map/all_to_all | solution.py:284
  77.8 0.6 copy-start.8
  81.3 11.7 %all-to-all-start.4 = ((f32[32,8,128]{2,1,0:T(8,128)}), f32[32,8,128]{2,1,0:T(8,128)S(1)}, u32[]{:S(2)}, u32[]{:S(2)}) async-start(f32[32,8,128]{2,1,0:T(8,128)} %get-tuple-element.23), calls=%async_computation.4 | async-start | bytes 262144 | tf_op jit(solution)/shard_map/all_to_all | solution.py:284
  93.0 0.6 copy-start.5
  96.7 13.6 %all-to-all-start.5 = ((f32[8,16,128]{2,1,0:T(8,128)}), f32[8,16,128]{2,1,0:T(8,128)S(1)}, u32[]{:S(2)}, u32[]{:S(2)}) async-start(f32[8,16,128]{2,1,0:T(8,128)} %col_sums.3), calls=%async_computation.5 | async-start | bytes 131072 | tf_op jit(solution)/shard_map/all_to_all | solution.py:284
  101.1 1.3 copy-start
  110.3 3.5 %copy-start.10 = (f32[16,128]{1,0:T(8,128)S(1)}, f32[16,128]{1,0:T(8,128)}, u32[]{:S(2)}) copy-start(f32[16,128]{1,0:T(8,128)} %get-tuple-element.25) | copy-start | bytes 24580
  110.3 0.6 copy-start.7
  115.5 13.8 %all-to-all-start.6 = ((f32[32,24,128]{2,1,0:T(8,128)}), f32[32,24,128]{2,1,0:T(8,128)S(1)}, u32[]{:S(2)}, u32[]{:S(2)}) async-start(f32[32,24,128]{2,1,0:T(8,128)} %pad_maximum_fusion), calls=%async_computation.6 | async-start | bytes 786432 | tf_op jit(solution)/shard_map/all_to_all | solution.py:284
  151.0 10.3 %collective-permute-start.11 = (f32[4,8,2048]{2,1,0:T(8,128)S(1)}, f32[4,8,2048]{2,1,0:T(8,128)S(1)}, u32[]{:S(2)}, u32[]{:S(2)}) collective-permute-start(f32[4,8,2048]{2,1,0:T(8,128)S(1)} %get-tuple-element.44), channel_id=1, source_target_pairs={{0,8},{8,16},{16,24},{24,32},{32,40},{40,48},{48,56},{56,0},{1,9},... | collective-permute-start | bytes 786440 | tf_op jit(solution)/shard_map/ppermute | solution.py:280
  153.0 10.8 %collective-permute-start.15 = (f32[4,8,2048]{2,1,0:T(8,128)S(1)}, f32[4,8,2048]{2,1,0:T(8,128)S(1)}, u32[]{:S(2)}, u32[]{:S(2)}) collective-permute-start(f32[4,8,2048]{2,1,0:T(8,128)S(1)} %get-tuple-element.45), channel_id=1, source_target_pairs={{0,56},{8,0},{16,8},{24,16},{32,24},{40,32},{48,40},{56,48},{1,57}... | collective-permute-start | bytes 786440 | tf_op jit(solution)/shard_map/ppermute | solution.py:280
  156.6 21.0 %copy-start.1 = (f32[1920,128]{1,0:T(8,128)S(1)}, f32[1920,128]{1,0:T(8,128)}, u32[]{:S(2)}) copy-start(f32[1920,128]{1,0:T(8,128)} %get-tuple-element.29) | copy-start | bytes 2949124
  156.6 21.0 %copy-start.2 = (f32[1920,128]{1,0:T(8,128)S(1)}, f32[1920,128]{1,0:T(8,128)}, u32[]{:S(2)}) copy-start(f32[1920,128]{1,0:T(8,128)} %get-tuple-element.30) | copy-start | bytes 2949124
  156.6 21.0 %collective-permute-start.3 = (f32[1920,128]{1,0:T(8,128)}, f32[1920,128]{1,0:T(8,128)}, u32[]{:S(2)}, u32[]{:S(2)}) collective-permute-start(f32[1920,128]{1,0:T(8,128)} %broadcast_select_fusion), channel_id=1, source_target_pairs={{0,1},{1,0},{2,3},{3,2},{4,5},{5,4},{6,7},{7,6},{8,9},{9,8},{10,11... | collective-permute-start | bytes 2949128 | tf_op jit(solution)/shard_map/ppermute | solution.py:280
  163.0 9.5 %collective-permute-start.12 = (f32[4,8,2048]{2,1,0:T(8,128)}, f32[4,8,2048]{2,1,0:T(8,128)S(1)}, u32[]{:S(2)}, u32[]{:S(2)}) collective-permute-start(f32[4,8,2048]{2,1,0:T(8,128)} %bitcast_add_fusion.4), channel_id=1, source_target_pairs={{0,8},{8,16},{16,24},{24,32},{32,40},{40,48},{48,56},{56,0},{1,9},... | collective-permute-start | bytes 786440 | tf_op jit(solution)/shard_map/ppermute | solution.py:280
  174.4 8.8 %collective-permute-start.13 = (f32[4,8,2048]{2,1,0:T(8,128)}, f32[4,8,2048]{2,1,0:T(8,128)}, u32[]{:S(2)}, u32[]{:S(2)}) collective-permute-start(f32[4,8,2048]{2,1,0:T(8,128)} %get-tuple-element.42), channel_id=1, source_target_pairs={{0,8},{8,16},{16,24},{24,32},{32,40},{40,48},{48,56},{56,0},{1,9},... | collective-permute-start | bytes 786440 | tf_op jit(solution)/shard_map/ppermute | solution.py:280
  174.4 8.8 %collective-permute-start.16 = (f32[4,8,2048]{2,1,0:T(8,128)}, f32[4,8,2048]{2,1,0:T(8,128)}, u32[]{:S(2)}, u32[]{:S(2)}) collective-permute-start(f32[4,8,2048]{2,1,0:T(8,128)} %get-tuple-element.43), channel_id=1, source_target_pairs={{0,56},{8,0},{16,8},{24,16},{32,24},{40,32},{48,40},{56,48},{1,57}... | collective-permute-start | bytes 786440 | tf_op jit(solution)/shard_map/ppermute | solution.py:280
  179.8 11.0 %collective-permute-start.4 = (f32[240,128]{0,1:T(8,128)}, f32[240,128]{0,1:T(8,128)S(1)}, u32[]{:S(2)}, u32[]{:S(2)}) collective-permute-start(f32[240,128]{0,1:T(8,128)} %bitcast.9), channel_id=1, source_target_pairs={{0,64},{64,128},{128,192},{192,0},{1,65},{65,129},{129,193},{193,1... | collective-permute-start | bytes 368648 | tf_op jit(solution)/shard_map/ppermute | solution.py:280
  185.1 12.1 %collective-permute-start.14 = (f32[4,8,2048]{2,1,0:T(8,128)}, f32[4,8,2048]{2,1,0:T(8,128)S(1)}, u32[]{:S(2)}, u32[]{:S(2)}) collective-permute-start(f32[4,8,2048]{2,1,0:T(8,128)} %get-tuple-element.40), channel_id=1, source_target_pairs={{0,8},{8,16},{16,24},{24,32},{32,40},{40,48},{48,56},{56,0},{1,9},... | collective-permute-start | bytes 786440 | tf_op jit(solution)/shard_map/ppermute | solution.py:280
  185.4 11.9 %collective-permute-start.17 = (f32[4,8,2048]{2,1,0:T(8,128)S(1)}, f32[4,8,2048]{2,1,0:T(8,128)}, u32[]{:S(2)}, u32[]{:S(2)}) collective-permute-start(f32[4,8,2048]{2,1,0:T(8,128)S(1)} %get-tuple-element.41), channel_id=1, source_target_pairs={{0,56},{8,0},{16,8},{24,16},{32,24},{40,32},{48,40},{56,48},{1,57}... | collective-permute-start | bytes 786440 | tf_op jit(solution)/shard_map/ppermute | solution.py:280
  189.0 5.4 %collective-permute-start.6 = (f32[240,128]{0,1:T(8,128)S(1)}, f32[240,128]{0,1:T(8,128)S(1)}, u32[]{:S(2)}, u32[]{:S(2)}) collective-permute-start(f32[240,128]{0,1:T(8,128)S(1)} %bitcast.80), channel_id=1, source_target_pairs={{0,192},{64,0},{128,64},{192,128},{1,193},{65,1},{129,65},{193,129... | collective-permute-start | bytes 368648 | tf_op jit(solution)/shard_map/ppermute | solution.py:280
  191.0 11.5 %collective-permute-start.5 = (f32[480,128]{0,1:T(8,128)S(1)}, f32[480,128]{0,1:T(8,128)S(1)}, u32[]{:S(2)}, u32[]{:S(2)}) collective-permute-start(f32[480,128]{0,1:T(8,128)S(1)} %pad_maximum_fusion.1), channel_id=1, source_target_pairs={{0,64},{64,128},{128,192},{192,0},{1,65},{65,129},{129,193},{193,1... | collective-permute-start | bytes 737288 | tf_op jit(solution)/shard_map/ppermute | solution.py:280
  194.6 7.9 %collective-permute-start.7 = (f32[480,128]{0,1:T(8,128)S(1)}, f32[480,128]{0,1:T(8,128)S(1)}, u32[]{:S(2)}, u32[]{:S(2)}) collective-permute-start(f32[480,128]{0,1:T(8,128)S(1)} %pad_maximum_fusion.2), channel_id=1, source_target_pairs={{0,192},{64,0},{128,64},{192,128},{1,193},{65,1},{129,65},{193,129... | collective-permute-start | bytes 737288 | tf_op jit(solution)/shard_map/ppermute | solution.py:280
  199.0 10.1 %all-to-all-start.8 = ((f32[4,8,2048]{2,1,0:T(8,128)}), f32[4,8,2048]{2,1,0:T(8,128)S(1)}, u32[]{:S(2)}, u32[]{:S(2)}) async-start(f32[4,8,2048]{2,1,0:T(8,128)} %fusion), calls=%async_computation.8 | async-start | bytes 524288 | tf_op jit(solution)/shard_map/all_to_all | solution.py:284
  203.1 7.1 %collective-permute-start.8 = (f32[480,32]{1,0:T(8,128)S(1)}, f32[480,32]{1,0:T(8,128)S(1)}, u32[]{:S(2)}, u32[]{:S(2)}) collective-permute-start(f32[480,32]{1,0:T(8,128)S(1)} %bitcast.79), channel_id=1, source_target_pairs={{0,2},{2,4},{4,6},{6,0},{1,3},{3,5},{5,7},{7,1},{8,10},{10,12},{12... | collective-permute-start | bytes 184328 | tf_op jit(solution)/shard_map/ppermute | solution.py:280
  203.1 7.6 %collective-permute-start.9 = (f32[480,32]{1,0:T(8,128)S(1)}, f32[480,32]{1,0:T(8,128)S(1)}, u32[]{:S(2)}, u32[]{:S(2)}) collective-permute-start(f32[480,32]{1,0:T(8,128)S(1)} %bitcast.78), channel_id=1, source_target_pairs={{0,6},{2,0},{4,2},{6,4},{1,7},{3,1},{5,3},{7,5},{8,14},{10,8},{12,... | collective-permute-start | bytes 184328 | tf_op jit(solution)/shard_map/ppermute | solution.py:280
  205.2 8.3 %collective-permute-start.10 = (f32[480,32]{1,0:T(8,128)S(1)}, f32[480,32]{1,0:T(8,128)S(1)}, u32[]{:S(2)}, u32[]{:S(2)}) collective-permute-start(f32[480,32]{1,0:T(8,128)S(1)} %bitcast.77), channel_id=1, source_target_pairs={{0,4},{2,6},{4,0},{6,2},{1,5},{3,7},{5,1},{7,3},{8,12},{10,14},{12... | collective-permute-start | bytes 184328 | tf_op jit(solution)/shard_map/ppermute | solution.py:280
  214.3 9.3 %all-to-all-start.7 = ((f32[8,8,128]{2,1,0:T(8,128)}), f32[8,8,128]{2,1,0:T(8,128)S(1)}, u32[]{:S(2)}, u32[]{:S(2)}) async-start(f32[8,8,128]{2,1,0:T(8,128)} %broadcast_in_dim.44), calls=%async_computation.7 | async-start | bytes 65536 | tf_op jit(solution)/shard_map/all_to_all | solution.py:284
